TPU v7x, 256 devices: a whole 4x4x8 slice. The times are simulated.
256 devices in a mesh: win: 4 (over y_lo, core), tile: 64 (over x, y_hi, z).
Axes of the slice: x: 4, y: 4 (y_hi: 2, y_lo: 2; y = y_hi * 2 + y_lo), z: 8, core: 2. Of those that a mesh axis runs over, the one named last changes fastest.
Arguments:
- state: float32 [4, 64, 5, 32, 8, 128], P('win', 'tile'), may hold values from -6 to 6
- obs_weight: float32 [4, 64, 5, 32, 8, 128], P('win', 'tile'), may hold values from 0 to 1
- trajectory: bfloat16 [4, 64, 3, 2, 32, 8, 128], P('win', 'tile'), may hold values from -0.8984375 to 0.8984375
- coupling: float32 [5, 5], replicated, may hold values from -0.9 to 0.9
- prec_scale: float32 [5, 32], replicated, may hold values from 0.5 to 2
Outputs:
- hess_vec: float32 [4, 64, 5, 32, 8, 128], P('win', 'tile')
All inputs are finite; a program needn't handle non-finite values.
Results may differ from a plain program's by a relative error of at most 0.0003.
Values sent between devices are 32-bit elements; how exact they have to be, the bound alone decides.
No kernel may reach another device: no remote copies, remote signals or barrier semaphores. Data moves between devices by JAX's collectives and lax.ppermute only.
A program may use at most 64 MiB of HBM per device.

v0:
```python
import functools

import jax
import jax.numpy as jnp
from jax import lax
from jax.experimental import pallas as pl
from jax.experimental.pallas import tpu as pltpu
from jax.sharding import PartitionSpec as P

VARS = 5
STEPS = 3
GROUP = 16
HALO = 5
TY = 4
OFF = 9
PADDED = OFF + GROUP + OFF
smooth_weight = 0.2


def passed_along(x, axis, by):
    devices = lax.axis_size(axis)
    pairs = [(i, i + by) for i in range(devices) if 0 <= i + by < devices]
    return lax.ppermute(x, axis, pairs)


def shifted(x, axis, by):
    devices = lax.axis_size(axis)
    return lax.ppermute(x, axis, [(i, (i + by) % devices) for i in range(devices)])


def exchange(x):
    groups = [[first + i for i in range(GROUP)] for first in range(0, lax.axis_size("tile"), GROUP)]
    return lax.all_to_all(x, "tile", 0, 0, axis_index_groups=groups, tiled=True)


def masks():
    row = lax.broadcasted_iota(jnp.int32, (8, 128), 0)
    lane = lax.broadcasted_iota(jnp.int32, (8, 128), 1)
    return row == 0, row == 7, lane == 0, lane == 127


def east(sel, here, there):
    return pltpu.roll(jnp.where(sel[0], there, here), 7, 0)


def west(sel, here, there):
    return pltpu.roll(jnp.where(sel[1], there, here), 1, 0)


def north(sel, here, there):
    return pltpu.roll(jnp.where(sel[2], there, here), 127, 1)


def south(sel, here, there):
    return pltpu.roll(jnp.where(sel[3], there, here), 1, 1)


def mixed(coupling, values, a, transposed):
    terms = [(coupling[b, a] if transposed else coupling[a, b]) * values[b] for b in range(VARS)]
    return ((terms[0] + terms[1]) + (terms[2] + terms[3])) + terms[4]


def tangent_step(levels, sel, coupling, src, winds, step, first, last, emit):
    @pl.loop(first, last)
    def _(i):
        for lv in range(levels):
            u = winds[i, (2 * step) * levels + lv]
            v = winds[i, (2 * step + 1) * levels + lv]
            f = [src[i, a * levels + lv] for a in range(VARS)]
            for a in range(VARS):
                k = a * levels + lv
                dx = east(sel, f[a], src[i + TY, k]) - west(sel, f[a], src[i - TY, k])
                dy = north(sel, f[a], src[i + 1, k]) - south(sel, f[a], src[i - 1, k])
                emit(i, k, (f[a] + mixed(coupling, f, a, False)) + (u * dx + v * dy))


def adjoint_step(levels, sel, coupling, src, winds, step, first, last, emit):
    @pl.loop(first, last)
    def _(i):
        for lv in range(levels):
            ku = (2 * step) * levels + lv
            kv = (2 * step + 1) * levels + lv
            ue = east(sel, winds[i, ku], winds[i + TY, ku])
            uw = west(sel, winds[i, ku], winds[i - TY, ku])
            vn = north(sel, winds[i, kv], winds[i + 1, kv])
            vs = south(sel, winds[i, kv], winds[i - 1, kv])
            g = [src[i, a * levels + lv] for a in range(VARS)]
            for a in range(VARS):
                k = a * levels + lv
                flux = uw * west(sel, g[a], src[i - TY, k]) - ue * east(sel, g[a], src[i + TY, k])
                flux += vs * south(sel, g[a], src[i - 1, k]) - vn * north(sel, g[a], src[i + 1, k])
                emit(i, k, (g[a] + mixed(coupling, g, a, True)) + flux)


def precision_step(levels, sel, prec, src, first, last, emit):
    @pl.loop(first, last)
    def _(i):
        for lv in range(levels):
            for a in range(VARS):
                k = a * levels + lv
                f = src[i, k]
                around = east(sel, f, src[i + TY, k]) + west(sel, f, src[i - TY, k])
                around += north(sel, f, src[i + 1, k]) + south(sel, f, src[i - 1, k])
                emit(i, k, prec[a, lv] * ((1.0 + 4.0 * smooth_weight) * f - smooth_weight * around))


def gather_tiles(parts, dst, sems, base):
    west_part, own, east_part = parts
    copies = [
        pltpu.make_async_copy(west_part, dst.at[pl.ds(OFF - HALO, HALO)], sems.at[base]),
        pltpu.make_async_copy(own, dst.at[pl.ds(OFF, GROUP)], sems.at[base + 1]),
        pltpu.make_async_copy(east_part, dst.at[pl.ds(OFF + GROUP, HALO)], sems.at[base + 2]),
    ]
    for copy in copies:
        copy.start()
    return copies


LO, HI = OFF - HALO, OFF + GROUP + HALO


def forward_kernel(levels, window, coupling, prec, sw, so, se, ww, wo, we, fw, fo, fe,
                   full, core, own_weighted, f0, f1, winds, follow, sems):
    sel = masks()
    state_copies = gather_tiles((sw, so, se), f0, sems, 0)
    wind_copies = gather_tiles((ww, wo, we), winds, sems, 3)
    follow_copies = gather_tiles((fw, fo, fe), follow, sems, 6)
    for copy in state_copies + wind_copies + follow_copies:
        copy.wait()

    @pl.when(window[0] == 0)
    def _():
        def emit(i, k, value):
            own_weighted[i - OFF, k] = value

        precision_step(levels, sel, prec, f0, OFF, OFF + GROUP, emit)

    @pl.when(window[0] == window[1])
    def _():
        full[...] = jnp.zeros_like(full)
        core[...] = jnp.zeros_like(core)

    @pl.when(window[0] != window[1])
    def _():
        def into(ref):
            def emit(i, k, value):
                ref[i, k] = value

            return emit

        def mismatch(i, k, value):
            f1[i, k] = follow[i, k] - value

        def weigh(i, k, value):
            full[i - LO, k] = value

        tangent_step(levels, sel, coupling, f0, winds, 0, LO, HI, into(f1))
        tangent_step(levels, sel, coupling, f1, winds, 1, LO, HI, into(f0))
        tangent_step(levels, sel, coupling, f0, winds, 2, LO, HI, mismatch)
        precision_step(levels, sel, prec, f1, LO, HI, weigh)
        core[...] = full[pl.ds(HALO, GROUP)]


def backward_kernel(levels, window, coupling, weighted, ww, wo, we, out, f0, f1, winds, sems):
    sel = masks()
    copies = gather_tiles((ww, wo, we), winds, sems, 0)
    own = pltpu.make_async_copy(weighted, f0.at[pl.ds(LO, HI - LO)], sems.at[3])
    own.start()
    for copy in copies + [own]:
        copy.wait()

    @pl.when(window[0] == window[1])
    def _():
        out[...] = jnp.zeros_like(out)

    @pl.when(window[0] != window[1])
    def _():
        def into(ref):
            def emit(i, k, value):
                ref[i, k] = value

            return emit

        def result(i, k, value):
            out[i - OFF, k] = value

        adjoint_step(levels, sel, coupling, f0, winds, 2, LO, HI, into(f1))
        adjoint_step(levels, sel, coupling, f1, winds, 1, LO + 1, HI - 1, into(f0))
        adjoint_step(levels, sel, coupling, f0, winds, 0, OFF, OFF + GROUP, result)


def with_halo(x):
    return shifted(x[GROUP - HALO :], "tile", GROUP), x, shifted(x[:HALO], "tile", -GROUP)


def body(state, obs_weight, trajectory, coupling, prec_scale):
    own_state = state[0, 0]
    level_count = own_state.shape[1]
    levels = level_count // GROUP
    cell = own_state.shape[2:]
    window_index = lax.axis_index("win")
    last_window = lax.axis_size("win") - 1
    window = jnp.stack([window_index, jnp.int32(last_window)]).astype(jnp.int32)
    first_level = (lax.axis_index("tile") % GROUP) * levels
    prec = lax.dynamic_slice_in_dim(prec_scale, first_level, levels, axis=1)

    def by_level(x):
        kinds = x.shape[0]
        x = x.reshape((kinds, GROUP, levels) + cell)
        return jnp.moveaxis(x, 1, 0).reshape((GROUP, kinds * levels) + cell)

    slab = exchange(by_level(own_state))
    slab_parts = with_halo(slab)
    follow_core = passed_along(slab, "win", -1)
    winds = exchange(by_level(trajectory[0, 0].reshape((2 * STEPS, level_count) + cell).astype(jnp.float32)))
    wind_parts = with_halo(winds)
    follow_parts = (passed_along(slab_parts[0], "win", -1), follow_core, passed_along(slab_parts[2], "win", -1))

    fields = VARS * levels
    smem = pl.BlockSpec(memory_space=pltpu.SMEM)
    anyspace = pl.BlockSpec(memory_space=pl.ANY)
    vmem = pl.BlockSpec(memory_space=pltpu.VMEM)
    padded = pltpu.VMEM((PADDED, fields) + cell, jnp.float32)
    padded_winds = pltpu.VMEM((PADDED, 2 * STEPS * levels) + cell, jnp.float32)
    core_shape = jax.ShapeDtypeStruct((GROUP, fields) + cell, jnp.float32)
    full_shape = jax.ShapeDtypeStruct((HI - LO, fields) + cell, jnp.float32)
    full, core, own_weighted = pl.pallas_call(
        functools.partial(forward_kernel, levels),
        out_shape=(full_shape, core_shape, core_shape),
        in_specs=[smem] * 3 + [anyspace] * 9,
        out_specs=(vmem,) * 3,
        scratch_shapes=[padded, padded, padded_winds, padded, pltpu.SemaphoreType.DMA((9,))],
        compiler_params=pltpu.CompilerParams(vmem_limit_bytes=40 * 2**20),
        name="forward",
    )(window, coupling, prec, *slab_parts, *wind_parts, *follow_parts)
    earlier = passed_along(core, "win", 1)
    cotangent = pl.pallas_call(
        functools.partial(backward_kernel, levels),
        out_shape=core_shape,
        in_specs=[smem] * 2 + [anyspace] * 4,
        out_specs=vmem,
        scratch_shapes=[padded, padded, padded_winds, pltpu.SemaphoreType.DMA((4,))],
        compiler_params=pltpu.CompilerParams(vmem_limit_bytes=40 * 2**20),
        cost_estimate=pl.CostEstimate(flops=20_000_000, bytes_accessed=4_000_000, transcendentals=0),
        name="backward",
    )(window, coupling, full, *wind_parts)
    weighted = jnp.where(window_index == 0, own_weighted, earlier)
    back = exchange(weighted - cotangent)
    back = jnp.moveaxis(back.reshape((GROUP, VARS, levels) + cell), 0, 1).reshape(own_state.shape)
    return (back + obs_weight[0, 0] * own_state)[None, None]


def solution(mesh):
    in_specs = (
        P("win", "tile", None, None, None, None),
        P("win", "tile", None, None, None, None),
        P("win", "tile", None, None, None, None, None),
        P(),
        P(),
    )
    out_specs = P("win", "tile", None, None, None, None)
    return jax.shard_map(body, mesh=mesh, in_specs=in_specs, out_specs=out_specs, check_vma=False)
```

profile of v0, /device:TPU:1, one launch (start us, length us, event | category | flops | bytes accessed | tf_op | source)
XLA Modules:
  0.0 127.3 jit_solution(16274240764798963665)
XLA Ops:
  0.0 2.0 %copy.6 = f32[5,16,2,8,128]{4,3,2,0,1:T(8,128)} copy(f32[5,16,2,8,128]{4,3,2,1,0:T(8,128)} %bitcast.14) | data formatting | bytes 1310720 | tf_op jit(solution)/shard_map/reshape;squeeze | solution.py:209
  2.0 11.7 %all-to-all-start = ((f32[16,10,8,128]{3,2,1,0:T(8,128)}), f32[16,10,8,128]{3,2,1,0:T(8,128)S(1)}, u32[]{:S(2)}, u32[]{:S(2)}) async-start(f32[16,10,8,128]{3,2,1,0:T(8,128)} %bitcast.3), calls=%async_computation | async-start | bytes 1310720 | tf_op jit(solution)/shard_map/all_to_all | solution.py:33
  13.8 1.0 copy.7
  14.8 17.6 %all-to-all-done.so = f32[16,10,8,128]{3,2,1,0:T(8,128)S(1)} async-done(((f32[16,10,8,128]{3,2,1,0:T(8,128)}), f32[16,10,8,128]{3,2,1,0:T(8,128)S(1)}, u32[]{:S(2)}, u32[]{:S(2)}) %all-to-all-start) | async-done | bytes 655392 | tf_op jit(solution)/shard_map/all_to_all | solution.py:33
  32.3 6.0 %all-to-all-start.1 = ((f32[16,12,8,128]{3,2,1,0:T(8,128)}), f32[16,12,8,128]{3,2,1,0:T(8,128)S(1)}, u32[]{:S(2)}, u32[]{:S(2)}) async-start(f32[16,12,8,128]{3,2,1,0:T(8,128)} %bitcast.6), calls=%async_computation.1 | async-start | bytes 1572864 | tf_op jit(solution)/shard_map/all_to_all | solution.py:33
  38.3 2.9 %collective-permute-start.5 = (f32[16,10,8,128]{3,2,1,0:T(8,128)S(1)}, f32[16,10,8,128]{3,2,1,0:T(8,128)S(1)}, u32[]{:S(2)}, u32[]{:S(2)}) collective-permute-start(f32[16,10,8,128]{3,2,1,0:T(8,128)S(1)} %all-to-all-done.so), channel_id=1, source_target_pairs={{64,0},{128,64},{192,128},{65,1},{129,65},{193,129},{66,2},{130,66... | collective-permute-start | bytes 1966088 | tf_op jit(solution)/shard_map/ppermute | solution.py:23
  41.2 0.8 fusion.1
  42.0 2.5 %collective-permute-start.1 = (f32[5,10,8,128]{3,2,1,0:T(8,128)}, f32[5,10,8,128]{3,2,1,0:T(8,128)S(1)}, u32[]{:S(2)}, u32[]{:S(2)}) collective-permute-start(f32[5,10,8,128]{3,2,1,0:T(8,128)} %get-tuple-element.13), channel_id=1, source_target_pairs={{0,48},{1,49},{2,50},{3,51},{4,52},{5,53},{6,54},{7,55},{8,56},{9,... | collective-permute-start | bytes 614408 | tf_op jit(solution)/shard_map/ppermute | solution.py:28
  44.5 14.8 %all-to-all-done.1.wo = f32[16,12,8,128]{3,2,1,0:T(8,128)S(1)} async-done(((f32[16,12,8,128]{3,2,1,0:T(8,128)}), f32[16,12,8,128]{3,2,1,0:T(8,128)S(1)}, u32[]{:S(2)}, u32[]{:S(2)}) %all-to-all-start.1) | async-done | bytes 786464 | tf_op jit(solution)/shard_map/all_to_all | solution.py:33
  59.3 0.7 fusion
  60.0 2.5 %collective-permute-start.3 = (f32[5,12,8,128]{3,2,1,0:T(8,128)}, f32[5,12,8,128]{3,2,1,0:T(8,128)S(1)}, u32[]{:S(2)}, u32[]{:S(2)}) collective-permute-start(f32[5,12,8,128]{3,2,1,0:T(8,128)} %get-tuple-element.11), channel_id=1, source_target_pairs={{0,48},{1,49},{2,50},{3,51},{4,52},{5,53},{6,54},{7,55},{8,56},{9,... | collective-permute-start | bytes 737288 | tf_op jit(solution)/shard_map/ppermute | solution.py:28
  62.5 4.7 %collective-permute-start.6 = (f32[5,10,8,128]{3,2,1,0:T(8,128)S(1)}, f32[5,10,8,128]{3,2,1,0:T(8,128)S(1)}, u32[]{:S(2)}, u32[]{:S(2)}) collective-permute-start(f32[5,10,8,128]{3,2,1,0:T(8,128)S(1)} %collective-permute-done.1.se), channel_id=1, source_target_pairs={{64,0},{128,64},{192,128},{65,1},{129,65},{193,129},{66,2},{130,66... | collective-permute-start | bytes 614408 | tf_op jit(solution)/shard_map/ppermute | solution.py:23
  67.2 1.9 %collective-permute-start.4 = (f32[5,10,8,128]{3,2,1,0:T(8,128)S(1)}, f32[5,10,8,128]{3,2,1,0:T(8,128)S(1)}, u32[]{:S(2)}, u32[]{:S(2)}) collective-permute-start(f32[5,10,8,128]{3,2,1,0:T(8,128)S(1)} %collective-permute-done.sw), channel_id=1, source_target_pairs={{64,0},{128,64},{192,128},{65,1},{129,65},{193,129},{66,2},{130,66... | collective-permute-start | bytes 614408 | tf_op jit(solution)/shard_map/ppermute | solution.py:23
  69.3 1.9 %collective-permute-done.6.fe = f32[5,10,8,128]{3,2,1,0:T(8,128)S(1)} collective-permute-done((f32[5,10,8,128]{3,2,1,0:T(8,128)S(1)}, f32[5,10,8,128]{3,2,1,0:T(8,128)S(1)}, u32[]{:S(2)}, u32[]{:S(2)}) %collective-permute-start.6) | collective-permute-done | bytes 204832 | tf_op jit(solution)/shard_map/ppermute | solution.py:23
  71.2 3.1 %collective-permute-done.4.fw = f32[5,10,8,128]{3,2,1,0:T(8,128)S(1)} collective-permute-done((f32[5,10,8,128]{3,2,1,0:T(8,128)S(1)}, f32[5,10,8,128]{3,2,1,0:T(8,128)S(1)}, u32[]{:S(2)}, u32[]{:S(2)}) %collective-permute-start.4) | collective-permute-done | bytes 204832 | tf_op jit(solution)/shard_map/ppermute | solution.py:23
  74.3 0.8 copy-done.1
  75.1 1.1 copy-done.2
  76.2 13.5 %forward.1 = (f32[26,10,8,128]{3,2,1,0:T(8,128)S(1)}, f32[16,10,8,128]{3,2,1,0:T(8,128)}, f32[16,10,8,128]{3,2,1,0:T(8,128)S(1)}) custom-call(s32[2]{0:T(128)S(1)} %pad_add_fusion.window, f32[5,5]{1,0:T(8,128)S(1)} %copy-done.5, f32[5,2]{1,0:T(8,128)S(1)} %constant_dynamic-slice_fusion.prec, f32[5,10,8,128]{3,2,1,0:T(8,128)S(1)} %collective-permute-done.sw, ...), custom_call_target="tpu_custom_call" | custom-call | tf_op jit(solution)/shard_map/forward/pallas_call | solution.py:227
  89.7 0.9 copy-done.3
  90.6 1.9 %collective-permute-start.7 = (f32[16,10,8,128]{3,2,1,0:T(8,128)}, f32[16,10,8,128]{3,2,1,0:T(8,128)}, u32[]{:S(2)}, u32[]{:S(2)}) collective-permute-start(f32[16,10,8,128]{3,2,1,0:T(8,128)} %get-tuple-element.9), channel_id=1, source_target_pairs={{0,64},{64,128},{128,192},{1,65},{65,129},{129,193},{2,66},{66,130... | collective-permute-start | bytes 1966088 | tf_op jit(solution)/shard_map/ppermute | solution.py:23
  92.5 7.9 %backward.1 = f32[16,10,8,128]{3,2,1,0:T(8,128)S(1)} custom-call(s32[2]{0:T(128)S(1)} %pad_add_fusion.window, f32[5,5]{1,0:T(8,128)S(1)} %copy-done.5, f32[26,10,8,128]{3,2,1,0:T(8,128)S(1)} %get-tuple-element.10.weighted, f32[5,12,8,128]{3,2,1,0:T(8,128)S(1)} %collective-permute-done.2.ww, f32[16,12,8,128]{3,2,1,0:T(8,128)S(1)} %all-to-all-done.1.wo, ...), custom_call_target="tpu_custom_call" | custom-call | flops 20000000 | bytes 4000000 | tf_op jit(solution)/shard_map/backward/pallas_call | solution.py:237
  100.5 1.2 select_subtract_fusion
  101.8 24.6 %all_to_all.15 = f32[16,10,8,128]{3,2,1,0:T(8,128)S(1)} all-to-all(f32[16,10,8,128]{3,2,1,0:T(8,128)S(1)} %select_subtract_fusion), channel_id=1, replica_groups={{0,1,2,3,4,5,6,7,8,9,10,11,12,13,14,15},{16,17,18,19,20,21,22,23,24,25,..., dimensions={0} | all-to-all | bytes 1310720 | tf_op jit(solution)/shard_map/all_to_all | solution.py:33
  126.4 0.9 multiply_add_fusion
  (26 shorter events, 0.3 us)
Async XLA Ops:
  0.0 69.2 %copy-start = (f32[5,32]{1,0:T(8,128)S(1)}, f32[5,32]{1,0:T(8,128)}, u32[]{:S(2)}) copy-start(f32[5,32]{1,0:T(8,128)} %param.9) | copy-start | bytes 1924
  0.0 13.8 %copy-start.8 = (bf16[1,1,3,2,32,8,128]{6,5,4,3,2,1,0:T(8,128)(2,1)S(1)}, bf16[1,1,3,2,32,8,128]{6,5,4,3,2,1,0:T(8,128)(2,1)}, u32[]{:S(2)}) copy-start(bf16[1,1,3,2,32,8,128]{6,5,4,3,2,1,0:T(8,128)(2,1)} %param.7) | copy-start | bytes 1179652
  2.0 30.3 %all-to-all-start = ((f32[16,10,8,128]{3,2,1,0:T(8,128)}), f32[16,10,8,128]{3,2,1,0:T(8,128)S(1)}, u32[]{:S(2)}, u32[]{:S(2)}) async-start(f32[16,10,8,128]{3,2,1,0:T(8,128)} %bitcast.3), calls=%async_computation | async-start | bytes 1310720 | tf_op jit(solution)/shard_map/all_to_all | solution.py:33
  32.3 27.0 %all-to-all-start.1 = ((f32[16,12,8,128]{3,2,1,0:T(8,128)}), f32[16,12,8,128]{3,2,1,0:T(8,128)S(1)}, u32[]{:S(2)}, u32[]{:S(2)}) async-start(f32[16,12,8,128]{3,2,1,0:T(8,128)} %bitcast.6), calls=%async_computation.1 | async-start | bytes 1572864 | tf_op jit(solution)/shard_map/all_to_all | solution.py:33
  38.3 36.9 %copy-start.5 = (f32[5,5]{1,0:T(8,128)S(1)}, f32[5,5]{1,0:T(8,128)}, u32[]{:S(2)}) copy-start(f32[5,5]{1,0:T(8,128)} %coupling.3) | copy-start | bytes 304
  38.3 36.0 %collective-permute-start.5 = (f32[16,10,8,128]{3,2,1,0:T(8,128)S(1)}, f32[16,10,8,128]{3,2,1,0:T(8,128)S(1)}, u32[]{:S(2)}, u32[]{:S(2)}) collective-permute-start(f32[16,10,8,128]{3,2,1,0:T(8,128)S(1)} %all-to-all-done.so), channel_id=1, source_target_pairs={{64,0},{128,64},{192,128},{65,1},{129,65},{193,129},{66,2},{130,66... | collective-permute-start | bytes 1966088 | tf_op jit(solution)/shard_map/ppermute | solution.py:23
  42.0 20.5 %collective-permute-start.1 = (f32[5,10,8,128]{3,2,1,0:T(8,128)}, f32[5,10,8,128]{3,2,1,0:T(8,128)S(1)}, u32[]{:S(2)}, u32[]{:S(2)}) collective-permute-start(f32[5,10,8,128]{3,2,1,0:T(8,128)} %get-tuple-element.13), channel_id=1, source_target_pairs={{0,48},{1,49},{2,50},{3,51},{4,52},{5,53},{6,54},{7,55},{8,56},{9,... | collective-permute-start | bytes 614408 | tf_op jit(solution)/shard_map/ppermute | solution.py:28
  44.5 22.7 %collective-permute-start = (f32[5,10,8,128]{3,2,1,0:T(8,128)}, f32[5,10,8,128]{3,2,1,0:T(8,128)S(1)}, u32[]{:S(2)}, u32[]{:S(2)}) collective-permute-start(f32[5,10,8,128]{3,2,1,0:T(8,128)} %get-tuple-element.14), channel_id=1, source_target_pairs={{0,16},{1,17},{2,18},{3,19},{4,20},{5,21},{6,22},{7,23},{8,24},{9,... | collective-permute-start | bytes 614408 | tf_op jit(solution)/shard_map/ppermute | solution.py:28
  60.0 14.3 %collective-permute-start.3 = (f32[5,12,8,128]{3,2,1,0:T(8,128)}, f32[5,12,8,128]{3,2,1,0:T(8,128)S(1)}, u32[]{:S(2)}, u32[]{:S(2)}) collective-permute-start(f32[5,12,8,128]{3,2,1,0:T(8,128)} %get-tuple-element.11), channel_id=1, source_target_pairs={{0,48},{1,49},{2,50},{3,51},{4,52},{5,53},{6,54},{7,55},{8,56},{9,... | collective-permute-start | bytes 737288 | tf_op jit(solution)/shard_map/ppermute | solution.py:28
  62.5 11.8 %collective-permute-start.2 = (f32[5,12,8,128]{3,2,1,0:T(8,128)S(1)}, f32[5,12,8,128]{3,2,1,0:T(8,128)S(1)}, u32[]{:S(2)}, u32[]{:S(2)}) collective-permute-start(f32[5,12,8,128]{3,2,1,0:T(8,128)S(1)} %get-tuple-element.12), channel_id=1, source_target_pairs={{0,16},{1,17},{2,18},{3,19},{4,20},{5,21},{6,22},{7,23},{8,24},{9,... | collective-permute-start | bytes 737288 | tf_op jit(solution)/shard_map/ppermute | solution.py:28
  62.5 8.7 %collective-permute-start.6 = (f32[5,10,8,128]{3,2,1,0:T(8,128)S(1)}, f32[5,10,8,128]{3,2,1,0:T(8,128)S(1)}, u32[]{:S(2)}, u32[]{:S(2)}) collective-permute-start(f32[5,10,8,128]{3,2,1,0:T(8,128)S(1)} %collective-permute-done.1.se), channel_id=1, source_target_pairs={{64,0},{128,64},{192,128},{65,1},{129,65},{193,129},{66,2},{130,66... | collective-permute-start | bytes 614408 | tf_op jit(solution)/shard_map/ppermute | solution.py:23
  67.2 7.1 %collective-permute-start.4 = (f32[5,10,8,128]{3,2,1,0:T(8,128)S(1)}, f32[5,10,8,128]{3,2,1,0:T(8,128)S(1)}, u32[]{:S(2)}, u32[]{:S(2)}) collective-permute-start(f32[5,10,8,128]{3,2,1,0:T(8,128)S(1)} %collective-permute-done.sw), channel_id=1, source_target_pairs={{64,0},{128,64},{192,128},{65,1},{129,65},{193,129},{66,2},{130,66... | collective-permute-start | bytes 614408 | tf_op jit(solution)/shard_map/ppermute | solution.py:23
  74.3 0.8 copy-start.1
  75.1 1.1 copy-start.2
  89.7 0.9 copy-start.3
  90.6 9.9 %collective-permute-start.7 = (f32[16,10,8,128]{3,2,1,0:T(8,128)}, f32[16,10,8,128]{3,2,1,0:T(8,128)}, u32[]{:S(2)}, u32[]{:S(2)}) collective-permute-start(f32[16,10,8,128]{3,2,1,0:T(8,128)} %get-tuple-element.9), channel_id=1, source_target_pairs={{0,64},{64,128},{128,192},{1,65},{65,129},{129,193},{2,66},{66,130... | collective-permute-start | bytes 1966088 | tf_op jit(solution)/shard_map/ppermute | solution.py:23
  92.5 8.0 %copy-start.4 = (f32[16,10,8,128]{3,2,1,0:T(8,128)S(1)}, f32[16,10,8,128]{3,2,1,0:T(8,128)}, u32[]{:S(2)}) copy-start(f32[16,10,8,128]{3,2,1,0:T(8,128)} %copy-done.3) | copy-start | bytes 1966084
  101.7 24.7 %copy-start.6 = (f32[1,1,5,32,8,128]{5,4,3,2,1,0:T(8,128)S(1)}, f32[1,1,5,32,8,128]{5,4,3,2,1,0:T(8,128)}, u32[]{:S(2)}) copy-start(f32[1,1,5,32,8,128]{5,4,3,2,1,0:T(8,128)} %param.5) | copy-start | bytes 1966084
  101.7 24.7 %copy-start.7 = (f32[1,1,5,32,8,128]{5,4,3,2,1,0:T(8,128)S(1)}, f32[1,1,5,32,8,128]{5,4,3,2,1,0:T(8,128)}, u32[]{:S(2)}) copy-start(f32[1,1,5,32,8,128]{5,4,3,2,1,0:T(8,128)} %param.6) | copy-start | bytes 1966084
where the time goes:
time: 129 us; the launch traced here: 127 us
  waiting for transfers between devices  37.3 us (29%)
  starting transfers between devices  34.1 us (26%)
  blocking collectives  24.6 us (19%)
  Pallas kernels  21.4 us (17%)
  local copies, waits for them, and re-layouts  7.44 us (6%)
  other arithmetic  2.23 us (2%)
    all_to_all x2, waiting for transfers between devices, exchange(): return lax.all_to_all(x, 'tile', 0, 0, axis_index_groups=groups, tiled=True)  32.3 us
    all_to_all x1, blocking collectives, exchange(): return lax.all_to_all(x, 'tile', 0, 0, axis_index_groups=groups, tiled=True)  24.6 us
    all_to_all x2, starting transfers between devices, exchange(): return lax.all_to_all(x, 'tile', 0, 0, axis_index_groups=groups, tiled=True)  17.7 us
    pallas_call x1, Pallas kernels, body(): pl.pallas_call(functools.partial(forward_kernel, levels), out_shape=(full...  13.5 us
    ppermute x4, starting transfers between devices, passed_along(): return lax.ppermute(x, axis, pairs)  11.4 us
    pallas_call x1, Pallas kernels, body(): pl.pallas_call(functools.partial(backward_kernel, levels), out_shape=core...  7.93 us
    ppermute x4, waiting for transfers between devices, passed_along(): return lax.ppermute(x, axis, pairs)  5 us
    ppermute x4, starting transfers between devices, shifted(): lax.ppermute(x, axis, [(i, (i + by) % devices) for i in range(devices)])  4.96 us
  transfers between devices with their start and end apart: 10, of which 4 were waited for; matrix products, arithmetic and copies ran while one was open for 2% of the time, Pallas kernels for 6%

commit v1 on v0

--- a/solution.py
+++ b/solution.py
@@ -14,6 +14,8 @@
 TY = 4
 OFF = 9
 PADDED = OFF + GROUP + OFF
+UNROLL = {26: 13, 24: 8, 16: 8}
+SPLIT = 1
 smooth_weight = 0.2
 
 
@@ -61,7 +63,7 @@
 
 
 def tangent_step(levels, sel, coupling, src, winds, step, first, last, emit):
-    @pl.loop(first, last)
+    @pl.loop(first, last, unroll=UNROLL[last - first])
     def _(i):
         for lv in range(levels):
             u = winds[i, (2 * step) * levels + lv]
@@ -75,7 +77,7 @@
 
 
 def adjoint_step(levels, sel, coupling, src, winds, step, first, last, emit):
-    @pl.loop(first, last)
+    @pl.loop(first, last, unroll=UNROLL[last - first])
     def _(i):
         for lv in range(levels):
             ku = (2 * step) * levels + lv
@@ -93,7 +95,7 @@
 
 
 def precision_step(levels, sel, prec, src, first, last, emit):
-    @pl.loop(first, last)
+    @pl.loop(first, last, unroll=UNROLL[last - first])
     def _(i):
         for lv in range(levels):
             for a in range(VARS):
@@ -104,8 +106,9 @@
                 emit(i, k, prec[a, lv] * ((1.0 + 4.0 * smooth_weight) * f - smooth_weight * around))
 
 
-def gather_tiles(parts, dst, sems, base):
-    west_part, own, east_part = parts
+def gather_tiles(parts, first, dst, sems, base):
+    planes = pl.ds(first, dst.shape[1])
+    west_part, own, east_part = [part.at[:, planes] for part in parts]
     copies = [
         pltpu.make_async_copy(west_part, dst.at[pl.ds(OFF - HALO, HALO)], sems.at[base]),
         pltpu.make_async_copy(own, dst.at[pl.ds(OFF, GROUP)], sems.at[base + 1]),
@@ -119,12 +122,13 @@
 LO, HI = OFF - HALO, OFF + GROUP + HALO
 
 
-def forward_kernel(levels, window, coupling, prec, sw, so, se, ww, wo, we, fw, fo, fe,
+def forward_kernel(levels, window, coupling, prec, west_in, own_in, east_in, fw, fo, fe,
                    full, core, own_weighted, f0, f1, winds, follow, sems):
     sel = masks()
-    state_copies = gather_tiles((sw, so, se), f0, sems, 0)
-    wind_copies = gather_tiles((ww, wo, we), winds, sems, 3)
-    follow_copies = gather_tiles((fw, fo, fe), follow, sems, 6)
+    parts = (west_in, own_in, east_in)
+    state_copies = gather_tiles(parts, 0, f0, sems, 0)
+    wind_copies = gather_tiles(parts, VARS * levels, winds, sems, 3)
+    follow_copies = gather_tiles((fw, fo, fe), 0, follow, sems, 6)
     for copy in state_copies + wind_copies + follow_copies:
         copy.wait()
 
@@ -161,9 +165,9 @@
         core[...] = full[pl.ds(HALO, GROUP)]
 
 
-def backward_kernel(levels, window, coupling, weighted, ww, wo, we, out, f0, f1, winds, sems):
+def backward_kernel(levels, window, coupling, weighted, west_in, own_in, east_in, out, f0, f1, winds, sems):
     sel = masks()
-    copies = gather_tiles((ww, wo, we), winds, sems, 0)
+    copies = gather_tiles((west_in, own_in, east_in), VARS * levels, winds, sems, 0)
     own = pltpu.make_async_copy(weighted, f0.at[pl.ds(LO, HI - LO)], sems.at[3])
     own.start()
     for copy in copies + [own]:
@@ -193,15 +197,14 @@
     return shifted(x[GROUP - HALO :], "tile", GROUP), x, shifted(x[:HALO], "tile", -GROUP)
 
 
-def body(state, obs_weight, trajectory, coupling, prec_scale):
-    own_state = state[0, 0]
-    level_count = own_state.shape[1]
-    levels = level_count // GROUP
+def chunk_apply(own_state, winds, coupling, prec_scale, half):
+    levels = own_state.shape[1] // GROUP
     cell = own_state.shape[2:]
+    fields = VARS * levels
     window_index = lax.axis_index("win")
     last_window = lax.axis_size("win") - 1
     window = jnp.stack([window_index, jnp.int32(last_window)]).astype(jnp.int32)
-    first_level = (lax.axis_index("tile") % GROUP) * levels
+    first_level = (half * GROUP + lax.axis_index("tile") % GROUP) * levels
     prec = lax.dynamic_slice_in_dim(prec_scale, first_level, levels, axis=1)
 
     def by_level(x):
@@ -209,14 +212,10 @@
         x = x.reshape((kinds, GROUP, levels) + cell)
         return jnp.moveaxis(x, 1, 0).reshape((GROUP, kinds * levels) + cell)
 
-    slab = exchange(by_level(own_state))
-    slab_parts = with_halo(slab)
-    follow_core = passed_along(slab, "win", -1)
-    winds = exchange(by_level(trajectory[0, 0].reshape((2 * STEPS, level_count) + cell).astype(jnp.float32)))
-    wind_parts = with_halo(winds)
-    follow_parts = (passed_along(slab_parts[0], "win", -1), follow_core, passed_along(slab_parts[2], "win", -1))
-
-    fields = VARS * levels
+    slab = exchange(by_level(jnp.concatenate([own_state, winds])))
+    parts = with_halo(slab)
+    follow_parts = [passed_along(part[:, :fields], "win", -1) for part in parts]
+
     smem = pl.BlockSpec(memory_space=pltpu.SMEM)
     anyspace = pl.BlockSpec(memory_space=pl.ANY)
     vmem = pl.BlockSpec(memory_space=pltpu.VMEM)
@@ -227,12 +226,13 @@
     full, core, own_weighted = pl.pallas_call(
         functools.partial(forward_kernel, levels),
         out_shape=(full_shape, core_shape, core_shape),
-        in_specs=[smem] * 3 + [anyspace] * 9,
+        in_specs=[smem] * 3 + [anyspace] * 6,
         out_specs=(vmem,) * 3,
         scratch_shapes=[padded, padded, padded_winds, padded, pltpu.SemaphoreType.DMA((9,))],
-        compiler_params=pltpu.CompilerParams(vmem_limit_bytes=40 * 2**20),
+        compiler_params=pltpu.CompilerParams(vmem_limit_bytes=24 * 2**20),
+        cost_estimate=pl.CostEstimate(flops=8_000_000 * levels, bytes_accessed=8_000_000 * levels, transcendentals=0),
         name="forward",
-    )(window, coupling, prec, *slab_parts, *wind_parts, *follow_parts)
+    )(window, coupling, prec, *parts, *follow_parts)
     earlier = passed_along(core, "win", 1)
     cotangent = pl.pallas_call(
         functools.partial(backward_kernel, levels),
@@ -240,13 +240,25 @@
         in_specs=[smem] * 2 + [anyspace] * 4,
         out_specs=vmem,
         scratch_shapes=[padded, padded, padded_winds, pltpu.SemaphoreType.DMA((4,))],
-        compiler_params=pltpu.CompilerParams(vmem_limit_bytes=40 * 2**20),
-        cost_estimate=pl.CostEstimate(flops=20_000_000, bytes_accessed=4_000_000, transcendentals=0),
+        compiler_params=pltpu.CompilerParams(vmem_limit_bytes=24 * 2**20),
+        cost_estimate=pl.CostEstimate(flops=6_000_000 * levels, bytes_accessed=6_000_000 * levels, transcendentals=0),
         name="backward",
-    )(window, coupling, full, *wind_parts)
+    )(window, coupling, full, *parts)
     weighted = jnp.where(window_index == 0, own_weighted, earlier)
     back = exchange(weighted - cotangent)
-    back = jnp.moveaxis(back.reshape((GROUP, VARS, levels) + cell), 0, 1).reshape(own_state.shape)
+    return jnp.moveaxis(back.reshape((GROUP, VARS, levels) + cell), 0, 1).reshape(own_state.shape)
+
+
+def body(state, obs_weight, trajectory, coupling, prec_scale):
+    own_state = state[0, 0]
+    level_count = own_state.shape[1]
+    winds = trajectory[0, 0].reshape((2 * STEPS,) + own_state.shape[1:]).astype(jnp.float32)
+    part = level_count // SPLIT
+    pieces = []
+    for half in range(SPLIT):
+        at = slice(half * part, (half + 1) * part)
+        pieces.append(chunk_apply(own_state[:, at], winds[:, at], coupling, prec_scale, half))
+    back = jnp.concatenate(pieces, axis=1)
     return (back + obs_weight[0, 0] * own_state)[None, None]
 
 

time: 129 us -> 117 us (0.907)
  blocking collectives: 24.6 us -> 71.4 us
  waiting for transfers between devices: 37.3 us -> 8.35 us
  starting transfers between devices: 34.1 us -> 18.3 us
  Pallas kernels: 21.4 us -> 9.61 us
  local copies, waits for them, and re-layouts: 7.44 us -> 4.98 us
    all_to_all x1 -> x2, blocking collectives: 24.6 us -> 71.4 us  [exchange(): return lax.all_to_all(x, 'tile', 0, 0, axis_index_groups=groups, tiled=True)]
    all_to_all x2 -> x0, waiting for transfers between devices: 32.3 us -> none  [exchange(): return lax.all_to_all(x, 'tile', 0, 0, axis_index_groups=groups, tiled=True)]
    all_to_all x2 -> x0, starting transfers between devices: 17.7 us -> none  [exchange(): return lax.all_to_all(x, 'tile', 0, 0, axis_index_groups=groups, tiled=True)]
    pallas_call x2, Pallas kernels: 21.4 us -> 9.61 us  [the longest x1 6.11 us: chunk_apply(): pl.pallas_call(functools.partial(forward_kernel, levels), out_shape=(full...]
    ppermute x4, starting transfers between devices: 11.4 us -> 15.8 us  [passed_along(): return lax.ppermute(x, axis, pairs)]
    ppermute x4 -> x2, starting transfers between devices: 4.96 us -> 2.48 us  [shifted(): lax.ppermute(x, axis, [(i, (i + by) % devices) for i in range(devices)])]
    ppermute x4, waiting for transfers between devices: 5 us -> 7.11 us  [passed_along(): return lax.ppermute(x, axis, pairs)]
    another operation x1 -> x0, local copies, waits for them, and re-layouts: 2.02 us -> none  [by_level(): x = x.reshape((kinds, GROUP, levels) + cell)]
  transfers between devices with their start and end apart: 10 -> 6, of which waited for: 4 -> 3; matrix products, arithmetic and copies ran while one was open for 2% -> 1% of each run, Pallas kernels for 6% -> 3%
where the time goes in v1:
time: 117 us; the launch traced here: 116 us
  blocking collectives  71.4 us (61%)
  starting transfers between devices  18.3 us (16%)
  Pallas kernels  9.61 us (8%)
  waiting for transfers between devices  8.35 us (7%)
  local copies, waits for them, and re-layouts  4.98 us (4%)
  other arithmetic  3.42 us (3%)
    all_to_all x2, blocking collectives, exchange(): return lax.all_to_all(x, 'tile', 0, 0, axis_index_groups=groups, tiled=True)  71.4 us
    ppermute x4, starting transfers between devices, passed_along(): return lax.ppermute(x, axis, pairs)  15.8 us
    ppermute x4, waiting for transfers between devices, passed_along(): return lax.ppermute(x, axis, pairs)  7.11 us
    pallas_call x1, Pallas kernels, chunk_apply(): pl.pallas_call(functools.partial(forward_kernel, levels), out_shape=(full...  6.11 us
    pallas_call x1, Pallas kernels, chunk_apply(): pl.pallas_call(functools.partial(backward_kernel, levels), out_shape=core...  3.5 us
    unnamed x18, local copies, waits for them, and re-layouts  2.88 us
    ppermute x2, starting transfers between devices, shifted(): lax.ppermute(x, axis, [(i, (i + by) % devices) for i in range(devices)])  2.48 us
  transfers between devices with their start and end apart: 6, of which 3 were waited for; matrix products, arithmetic and copies ran while one was open for 1% of the time, Pallas kernels for 3%

profile of v1, /device:TPU:1, one launch (start us, length us, event | category | flops | bytes accessed | tf_op | source)
XLA Modules:
  0.0 116.2 jit_solution(12534636572573210084)
XLA Ops:
  0.0 1.1 convert.1
  1.1 0.1 copy-done.6
  1.2 0.1 pad_maximum_fusion
  1.3 0.1 copy.9
  1.4 46.2 %all_to_all.10.own_in = f32[16,22,8,128]{3,2,1,0:T(8,128)S(1)} all-to-all(f32[16,22,8,128]{3,2,1,0:T(8,128)S(1)} %bitcast.11), channel_id=1, replica_groups={{0,1,2,3,4,5,6,7,8,9,10,11,12,13,14,15},{16,17,18,19,20,21,22,23,24,25,..., dimensions={0} | all-to-all | bytes 2883584 | tf_op jit(solution)/shard_map/all_to_all | solution.py:35
  47.7 1.0 fusion
  48.6 2.5 %collective-permute-start.1 = (f32[5,22,8,128]{3,2,1,0:T(8,128)}, f32[5,22,8,128]{3,2,1,0:T(8,128)S(1)}, u32[]{:S(2)}, u32[]{:S(2)}) collective-permute-start(f32[5,22,8,128]{3,2,1,0:T(8,128)} %get-tuple-element.11), channel_id=1, source_target_pairs={{0,48},{1,49},{2,50},{3,51},{4,52},{5,53},{6,54},{7,55},{8,56},{9,... | collective-permute-start | bytes 1351688 | tf_op jit(solution)/shard_map/ppermute | solution.py:30
  51.1 0.9 slice.23
  52.0 5.0 %collective-permute-start.3 = (f32[16,10,8,128]{3,2,1,0:T(8,128)}, f32[16,10,8,128]{3,2,1,0:T(8,128)S(1)}, u32[]{:S(2)}, u32[]{:S(2)}) collective-permute-start(f32[16,10,8,128]{3,2,1,0:T(8,128)} %slice.23), channel_id=1, source_target_pairs={{64,0},{128,64},{192,128},{65,1},{129,65},{193,129},{66,2},{130,66... | collective-permute-start | bytes 1966088 | tf_op jit(solution)/shard_map/ppermute | solution.py:25
  57.0 1.2 %collective-permute-done.1.east_in = f32[5,22,8,128]{3,2,1,0:T(8,128)S(1)} collective-permute-done((f32[5,22,8,128]{3,2,1,0:T(8,128)}, f32[5,22,8,128]{3,2,1,0:T(8,128)S(1)}, u32[]{:S(2)}, u32[]{:S(2)}) %collective-permute-start.1) | collective-permute-done | bytes 450592 | tf_op jit(solution)/shard_map/ppermute | solution.py:30
  58.3 5.6 %collective-permute-start.4 = (f32[5,10,8,128]{3,2,1,0:T(8,128)S(1)}, f32[5,10,8,128]{3,2,1,0:T(8,128)S(1)}, u32[]{:S(2)}, u32[]{:S(2)}) collective-permute-start(f32[5,10,8,128]{3,2,1,0:T(8,128)S(1)} %slice.24), channel_id=1, source_target_pairs={{64,0},{128,64},{192,128},{65,1},{129,65},{193,129},{66,2},{130,66... | collective-permute-start | bytes 614408 | tf_op jit(solution)/shard_map/ppermute | solution.py:25
  64.0 3.3 %collective-permute-start.2 = (f32[5,10,8,128]{3,2,1,0:T(8,128)S(1)}, f32[5,10,8,128]{3,2,1,0:T(8,128)S(1)}, u32[]{:S(2)}, u32[]{:S(2)}) collective-permute-start(f32[5,10,8,128]{3,2,1,0:T(8,128)S(1)} %slice.22), channel_id=1, source_target_pairs={{64,0},{128,64},{192,128},{65,1},{129,65},{193,129},{66,2},{130,66... | collective-permute-start | bytes 614408 | tf_op jit(solution)/shard_map/ppermute | solution.py:25
  67.2 0.1 pad_add_fusion.window
  67.4 0.8 copy-done.1
  68.2 2.8 %collective-permute-done.2.fw = f32[5,10,8,128]{3,2,1,0:T(8,128)S(1)} collective-permute-done((f32[5,10,8,128]{3,2,1,0:T(8,128)S(1)}, f32[5,10,8,128]{3,2,1,0:T(8,128)S(1)}, u32[]{:S(2)}, u32[]{:S(2)}) %collective-permute-start.2) | collective-permute-done | bytes 204832 | tf_op jit(solution)/shard_map/ppermute | solution.py:25
  71.0 1.1 copy-done.2
  72.1 6.1 %forward.1 = (f32[26,10,8,128]{3,2,1,0:T(8,128)S(1)}, f32[16,10,8,128]{3,2,1,0:T(8,128)}, f32[16,10,8,128]{3,2,1,0:T(8,128)S(1)}) custom-call(s32[2]{0:T(128)S(1)} %pad_add_fusion.window, f32[5,5]{1,0:T(8,128)S(1)} %copy-done.5, f32[5,2]{1,0:T(8,128)S(1)} %constant_dynamic-slice_fusion.prec, f32[5,22,8,128]{3,2,1,0:T(8,128)S(1)} %collective-permute-done.west_in, ...), custom_call_target="tpu_custom_call" | custom-call | flops 16000000 | bytes 16000000 | tf_op jit(solution)/shard_map/forward/pallas_call | solution.py:226
  78.3 0.8 copy-done.3
  79.1 1.9 %collective-permute-start.5 = (f32[16,10,8,128]{3,2,1,0:T(8,128)}, f32[16,10,8,128]{3,2,1,0:T(8,128)}, u32[]{:S(2)}, u32[]{:S(2)}) collective-permute-start(f32[16,10,8,128]{3,2,1,0:T(8,128)} %get-tuple-element.9), channel_id=1, source_target_pairs={{0,64},{64,128},{128,192},{1,65},{65,129},{129,193},{2,66},{66,130... | collective-permute-start | bytes 1966088 | tf_op jit(solution)/shard_map/ppermute | solution.py:25
  81.0 3.5 %backward.1 = f32[16,10,8,128]{3,2,1,0:T(8,128)S(1)} custom-call(s32[2]{0:T(128)S(1)} %pad_add_fusion.window, f32[5,5]{1,0:T(8,128)S(1)} %copy-done.5, f32[26,10,8,128]{3,2,1,0:T(8,128)S(1)} %get-tuple-element.10.weighted, f32[5,22,8,128]{3,2,1,0:T(8,128)S(1)} %collective-permute-done.west_in, f32[16,22,8,128]{3,2,1,0:T(8,128)S(1)} %all_to_all.10.own_in, ...), custom_call_target="tpu_custom_call" | custom-call | flops 12000000 | bytes 12000000 | tf_op jit(solution)/shard_map/backward/pallas_call | solution.py:237
  84.5 4.3 %collective-permute-done.5 = f32[16,10,8,128]{3,2,1,0:T(8,128)} collective-permute-done((f32[16,10,8,128]{3,2,1,0:T(8,128)}, f32[16,10,8,128]{3,2,1,0:T(8,128)}, u32[]{:S(2)}, u32[]{:S(2)}) %collective-permute-start.5) | collective-permute-done | bytes 655392 | tf_op jit(solution)/shard_map/ppermute | solution.py:25
  88.8 1.2 %select_subtract_fusion = f32[16,10,8,128]{3,2,1,0:T(8,128)S(1)} fusion(f32[16,10,8,128]{3,2,1,0:T(8,128)S(1)} %backward.1, f32[16,10,8,128]{3,2,1,0:T(8,128)S(1)} %copy-done.4, f32[16,10,8,128]{3,2,1,0:T(8,128)} %collective-permute-done.5, pred[]{:T(512)S(6)} %eq.5), kind=kLoop, calls=%fused_computation.2 | loop fusion | flops 327680 | bytes 2621441 | tf_op jit(solution)/shard_map/sub | solution.py:248
  90.1 25.2 %all_to_all.11 = f32[16,10,8,128]{3,2,1,0:T(8,128)S(1)} all-to-all(f32[16,10,8,128]{3,2,1,0:T(8,128)S(1)} %select_subtract_fusion), channel_id=1, replica_groups={{0,1,2,3,4,5,6,7,8,9,10,11,12,13,14,15},{16,17,18,19,20,21,22,23,24,25,..., dimensions={0} | all-to-all | bytes 1310720 | tf_op jit(solution)/shard_map/all_to_all | solution.py:35
  115.3 0.9 multiply_add_fusion
  (22 shorter events, 0.2 us)
Async XLA Ops:
  0.0 67.3 %copy-start = (f32[5,32]{1,0:T(8,128)S(1)}, f32[5,32]{1,0:T(8,128)}, u32[]{:S(2)}) copy-start(f32[5,32]{1,0:T(8,128)} %param.9) | copy-start | bytes 1924
  0.0 1.2 %copy-start.6 = (f32[1,1,5,32,8,128]{5,4,3,2,1,0:T(8,128)S(1)}, f32[1,1,5,32,8,128]{5,4,3,2,1,0:T(8,128)}, u32[]{:S(2)}) copy-start(f32[1,1,5,32,8,128]{5,4,3,2,1,0:T(8,128)} %param.5) | copy-start | bytes 1966084
  48.6 22.4 %copy-start.5 = (f32[5,5]{1,0:T(8,128)S(1)}, f32[5,5]{1,0:T(8,128)}, u32[]{:S(2)}) copy-start(f32[5,5]{1,0:T(8,128)} %coupling.3) | copy-start | bytes 304
  48.6 9.6 %collective-permute-start.1 = (f32[5,22,8,128]{3,2,1,0:T(8,128)}, f32[5,22,8,128]{3,2,1,0:T(8,128)S(1)}, u32[]{:S(2)}, u32[]{:S(2)}) collective-permute-start(f32[5,22,8,128]{3,2,1,0:T(8,128)} %get-tuple-element.11), channel_id=1, source_target_pairs={{0,48},{1,49},{2,50},{3,51},{4,52},{5,53},{6,54},{7,55},{8,56},{9,... | collective-permute-start | bytes 1351688 | tf_op jit(solution)/shard_map/ppermute | solution.py:30
  51.1 12.8 %collective-permute-start = (f32[5,22,8,128]{3,2,1,0:T(8,128)}, f32[5,22,8,128]{3,2,1,0:T(8,128)S(1)}, u32[]{:S(2)}, u32[]{:S(2)}) collective-permute-start(f32[5,22,8,128]{3,2,1,0:T(8,128)} %get-tuple-element.12), channel_id=1, source_target_pairs={{0,16},{1,17},{2,18},{3,19},{4,20},{5,21},{6,22},{7,23},{8,24},{9,... | collective-permute-start | bytes 1351688 | tf_op jit(solution)/shard_map/ppermute | solution.py:30
  52.0 15.4 %collective-permute-start.3 = (f32[16,10,8,128]{3,2,1,0:T(8,128)}, f32[16,10,8,128]{3,2,1,0:T(8,128)S(1)}, u32[]{:S(2)}, u32[]{:S(2)}) collective-permute-start(f32[16,10,8,128]{3,2,1,0:T(8,128)} %slice.23), channel_id=1, source_target_pairs={{64,0},{128,64},{192,128},{65,1},{129,65},{193,129},{66,2},{130,66... | collective-permute-start | bytes 1966088 | tf_op jit(solution)/shard_map/ppermute | solution.py:25
  58.3 10.0 %collective-permute-start.4 = (f32[5,10,8,128]{3,2,1,0:T(8,128)S(1)}, f32[5,10,8,128]{3,2,1,0:T(8,128)S(1)}, u32[]{:S(2)}, u32[]{:S(2)}) collective-permute-start(f32[5,10,8,128]{3,2,1,0:T(8,128)S(1)} %slice.24), channel_id=1, source_target_pairs={{64,0},{128,64},{192,128},{65,1},{129,65},{193,129},{66,2},{130,66... | collective-permute-start | bytes 614408 | tf_op jit(solution)/shard_map/ppermute | solution.py:25
  64.0 7.1 %collective-permute-start.2 = (f32[5,10,8,128]{3,2,1,0:T(8,128)S(1)}, f32[5,10,8,128]{3,2,1,0:T(8,128)S(1)}, u32[]{:S(2)}, u32[]{:S(2)}) collective-permute-start(f32[5,10,8,128]{3,2,1,0:T(8,128)S(1)} %slice.22), channel_id=1, source_target_pairs={{64,0},{128,64},{192,128},{65,1},{129,65},{193,129},{66,2},{130,66... | collective-permute-start | bytes 614408 | tf_op jit(solution)/shard_map/ppermute | solution.py:25
  67.4 0.8 copy-start.1
  71.0 1.1 copy-start.2
  78.2 0.8 copy-start.3
  79.1 9.7 %collective-permute-start.5 = (f32[16,10,8,128]{3,2,1,0:T(8,128)}, f32[16,10,8,128]{3,2,1,0:T(8,128)}, u32[]{:S(2)}, u32[]{:S(2)}) collective-permute-start(f32[16,10,8,128]{3,2,1,0:T(8,128)} %get-tuple-element.9), channel_id=1, source_target_pairs={{0,64},{64,128},{128,192},{1,65},{65,129},{129,193},{2,66},{66,130... | collective-permute-start | bytes 1966088 | tf_op jit(solution)/shard_map/ppermute | solution.py:25
  81.0 7.8 %copy-start.4 = (f32[16,10,8,128]{3,2,1,0:T(8,128)S(1)}, f32[16,10,8,128]{3,2,1,0:T(8,128)}, u32[]{:S(2)}) copy-start(f32[16,10,8,128]{3,2,1,0:T(8,128)} %copy-done.3) | copy-start | bytes 1966084
  90.0 25.3 %copy-start.7 = (f32[1,1,5,32,8,128]{5,4,3,2,1,0:T(8,128)S(1)}, f32[1,1,5,32,8,128]{5,4,3,2,1,0:T(8,128)}, u32[]{:S(2)}) copy-start(f32[1,1,5,32,8,128]{5,4,3,2,1,0:T(8,128)} %param.5) | copy-start | bytes 1966084
  90.0 25.3 %copy-start.8 = (f32[1,1,5,32,8,128]{5,4,3,2,1,0:T(8,128)S(1)}, f32[1,1,5,32,8,128]{5,4,3,2,1,0:T(8,128)}, u32[]{:S(2)}) copy-start(f32[1,1,5,32,8,128]{5,4,3,2,1,0:T(8,128)} %param.6) | copy-start | bytes 1966084
